TPU v7x, 128 devices: a whole 4x4x4 slice. The times are simulated.
128 devices in a mesh: dp: 128 (over x, z, y, core).
Axes of the slice: x: 4, y: 4, z: 4, core: 2. Of those that a mesh axis runs over, the one named last changes fastest.
Arguments:
- block_input: bfloat16 [16384, 512], P('dp')
- cotangent: bfloat16 [16384, 512], P('dp'), may hold values from -6 to 6
- segment_ids: int32 [128, 128], P('dp'), may hold values from 0 to 4, never falling along the last dimension, each value on 1 to 32 neighbouring positions
- attn_master: float32 [4, 512, 512], P(None, 'dp')
- up_master: float32 [512, 2048], P('dp'), may hold values from -0.25 to 0.25
- down_master: float32 [2048, 512], P('dp'), may hold values from -0.25 to 0.25
- vec_master: float32 [12, 512], P(None, 'dp')
- attn_moment: float32 [4, 512, 512], P(None, 'dp'), may hold values from -0.0078125 to 0.0078125
- up_moment: float32 [512, 2048], P('dp'), may hold values from -0.0078125 to 0.0078125
- down_moment: float32 [2048, 512], P('dp'), may hold values from -0.0078125 to 0.0078125
- vec_moment: float32 [12, 512], P(None, 'dp'), may hold values from -0.0024414062 to 0.0024414062
- vec_second: float32 [12, 512], P(None, 'dp'), may hold values from 1.4277229e-09 to 2.2843567e-08
Outputs:
- layer_out: bfloat16 [16384, 512], P('dp')
- input_grad: bfloat16 [16384, 512], P('dp')
- clip_norm: float32 [], replicated
- attn_momentum_new: float32 [4, 512, 512], P(None, 'dp')
- up_momentum_new: float32 [512, 2048], P('dp')
- down_momentum_new: float32 [2048, 512], P('dp')
- attn_new: float32 [4, 512, 512], P(None, 'dp')
- up_new: float32 [512, 2048], P('dp')
- down_new: float32 [2048, 512], P('dp')
- attn_copy: bfloat16 [4, 512, 512], P(None, 'dp')
- up_copy: bfloat16 [512, 2048], P('dp')
- down_copy: bfloat16 [2048, 512], P('dp')
- vec_moment_new: float32 [12, 512], P(None, 'dp')
- vec_second_new: float32 [12, 512], P(None, 'dp')
- vec_new: float32 [12, 512], P(None, 'dp')
- vec_copy: bfloat16 [12, 512], P(None, 'dp')
Inputs may be any that keep to these rules, and one draw needn't show every extreme that they name: `segment_ids`: in each packed row the sentence numbers start at 0 and never fall; each of the 5 sentences has 1 to 32 tokens, and one sentence of each row has exactly 32.
All inputs are finite; a program needn't handle non-finite values.
Results may differ from a plain program's by a relative error of at most 0.014.
The roundings to bfloat16 on the way count: a program that leaves them out, or rounds other values in their place, can miss the bound.
Values may be sent and summed in bfloat16 or wider, within the bound.
No kernel may reach another device: no remote copies, remote signals or barrier semaphores. Data moves between devices by JAX's collectives and lax.ppermute only.
A program may use at most 128 MiB of HBM per device.

v0:
```python
import math

import jax
import jax.numpy as jnp
from jax import lax
from jax.experimental import pallas as pl
from jax.experimental.pallas import tpu as pltpu
from jax.sharding import Mesh, PartitionSpec as P

D = 512
FF = 2048
H = 8
HD = 64
ROW = 128
STEP = 10
NS_ITERS = 5
HALF = 256

MASKED_SCORE = -1e30
NORM_EPSILON = 1e-05
CLIP_LIMIT = 1.0
MOMENTUM_DECAY = 0.95
RATE_MATRIX = 0.5
DECAY_MATRIX = 0.01
BETA_FIRST = 0.9
BETA_SECOND = 0.999
RATE_VECTOR = 0.2
ADAM_EPSILON = 1e-08
NEWTON_FIRST = 3.4445
NEWTON_SECOND = -4.775
NEWTON_THIRD = 2.0315

CHIPS = ("x", "z", "y")
ALL = ("x", "z", "y", "c")
BF = jnp.bfloat16
F32 = jnp.float32
VMEM_LIMIT = 12 * 1024 * 1024


def call(kernel, outs, ins, scratch=(), smem=(), args=(), far=(), results=(), away=(), flops=0, limit=VMEM_LIMIT):
    spec = [
        pl.BlockSpec(memory_space=pltpu.SMEM if i in smem else pl.ANY if i in far else pltpu.VMEM)
        for i in range(len(ins))
    ]
    placed = [
        x if i in smem or i in args
        else pltpu.with_memory_space_constraint(x, pltpu.HBM if i in far else pltpu.VMEM)
        for i, x in enumerate(ins)
    ]
    shapes = [
        jax.ShapeDtypeStruct(s, t) if i in results else pltpu.HBM(s, t) if i in away else pltpu.VMEM(s, t)
        for i, (s, t) in enumerate(outs)
    ]
    moved = sum(math.prod(a.shape) * a.dtype.itemsize for a in ins)
    return pl.pallas_call(
        kernel,
        out_shape=shapes,
        in_specs=spec,
        out_specs=[
            pl.BlockSpec(memory_space=pl.ANY if i in away else pltpu.VMEM) for i in range(len(shapes))
        ],
        scratch_shapes=list(scratch),
        compiler_params=pltpu.CompilerParams(vmem_limit_bytes=limit),
        cost_estimate=pl.CostEstimate(flops=flops, bytes_accessed=moved, transcendentals=0),
    )(*placed)


def dot(a, b):
    return jnp.dot(a, b, preferred_element_type=F32)


def dot_t(a, b):
    return lax.dot_general(a, b, (((1,), (1,)), ((), ())), preferred_element_type=F32)


def dot_in(a, b):
    return lax.dot_general(a, b, (((0,), (0,)), ((), ())), preferred_element_type=F32)


O_LANE, UP_LANE, DOWN_LANE, VEC_LANE, BLOCK = 768, 1024, 2048, 3072, 3200
X0, A0, H0, Z0, ACTS = 0, 512, 1024, 1536, 3328
Y0, DU0, DF0, GRADS = 0, 1024, 2048, 2560


def half_lanes(half, size):
    return pl.ds(pl.multiple_of(half * size, size), size)


def regroup():
    source = lax.broadcasted_iota(jnp.int32, (D, D), 0)
    target = lax.broadcasted_iota(jnp.int32, (D, D), 1)
    return jnp.where(target == (source & 3) * 128 + (source >> 2), 1.0, 0.0).astype(BF)


def pack_kernel(
    core, attn, up, down, vec, attn_m, up_m, down_m, keep, send,
    attn_v, up_v, down_v, vec_v, attn_mv, up_mv, down_mv, full, block, stage, sems,
):
    c = core[0]
    copies = [
        pltpu.make_async_copy(source, target, sems.at[i])
        for i, (source, target) in enumerate(
            [(attn, attn_v), (up, up_v), (down, down_v), (vec, vec_v), (attn_m, attn_mv), (up_m, up_mv), (down_m, down_mv)]
        )
    ]
    for copy in copies:
        copy.start()
    move = regroup()
    for copy in copies:
        copy.wait()
    for first, attn_one, up_one, down_one in ((0, attn_v, up_v, down_v), (4, attn_mv, up_mv, down_mv)):
        rows = slice(first, first + 4)
        for m in range(4):
            full[rows, D * m : D * (m + 1)] = attn_one[m]
        for part in range(4):
            row = 8 * part + first
            stage[row : row + 4, :] = up_one[:, D * part : D * (part + 1)]
        for i in range(4):
            for q in range(4):
                lane = 2 * FF + D * q
                full[first + i : first + i + 1, lane : lane + D] = down_one[4 * i + q : 4 * i + q + 1, :]
    moved = dot(stage[...].astype(BF), move)
    for part in range(4):
        for q in range(4):
            lane = FF + D * q + 128 * part
            full[:, lane : lane + 128] = moved[8 * part : 8 * (part + 1), 128 * q : 128 * (q + 1)]
    for target, half in ((keep, c), (send, 1 - c)):
        for m in range(4):
            lanes = pl.ds(pl.multiple_of(D * m + HALF * half, HALF), HALF)
            block[0:4, HALF * m : HALF * (m + 1)] = full[0:4, lanes]
        for m in range(2):
            lanes = pl.ds(pl.multiple_of(2 * D * m + D * half, D), D)
            block[4:8, D * m : D * (m + 1)] = full[4:8, lanes]
        block[:, UP_LANE:DOWN_LANE] = full[:, pl.ds(pl.multiple_of(FF + 1024 * half, 1024), 1024)]
        for q in range(4):
            lanes = pl.ds(pl.multiple_of(2 * FF + D * q + HALF * half, HALF), HALF)
            lane = DOWN_LANE + HALF * q
            block[0:4, lane : lane + HALF] = full[0:4, lanes]
        lanes = pl.ds(pl.multiple_of(2 * FF + 1024 * half, 1024), 1024)
        block[4:8, DOWN_LANE:VEC_LANE] = full[4:8, lanes]
        block[:, VEC_LANE:BLOCK] = jnp.zeros((8, 128), F32)
        block[0:4, VEC_LANE : VEC_LANE + 12] = vec_v[...]
        target[...] = block[...].astype(BF)


def role_lanes(block, note):
    gap = jnp.zeros((8, 512), block.dtype)
    tail = [] if note is None else [note]
    return [
        jnp.concatenate([block[:, 0:512], gap] + tail, axis=1),
        jnp.concatenate([block[:, 512:1024], gap] + tail, axis=1),
        jnp.concatenate([block[:, UP_LANE:DOWN_LANE]] + tail, axis=1),
        jnp.concatenate([block[:, DOWN_LANE:VEC_LANE]] + tail, axis=1),
    ]


def spread_kernel(core, keep, got, message, message_mom):
    mine, other = keep[...].astype(F32), got[...].astype(F32)
    is_left = core[0] == 0
    left, right = jnp.where(is_left, mine, other), jnp.where(is_left, other, mine)
    block = jnp.concatenate([left[0:4], right[0:4]], axis=0).astype(BF)
    moms = role_lanes(jnp.concatenate([left[4:8], right[4:8]], axis=0).astype(BF), None)
    for i in range(64):
        message[i] = block
        message_mom[i] = moms[i % 4]


def by_head(pair):
    low = (lax.broadcasted_iota(jnp.int32, (ROW, ROW), 1) < HD).astype(F32)
    return jnp.concatenate([pair * low.astype(BF), pair * (1.0 - low).astype(BF)], axis=0)


def abreast(stacked):
    return jnp.concatenate([stacked[0:ROW], stacked[ROW:]], axis=1)


def norm_parts(values):
    centred = values - jnp.mean(values, axis=-1, keepdims=True)
    scale = lax.rsqrt(jnp.mean(centred * centred, axis=-1, keepdims=True) + NORM_EPSILON)
    return centred * scale, scale


def norm_back(grad, gain, normed, scale):
    grad = grad * gain
    return scale * (
        grad
        - jnp.mean(grad, axis=-1, keepdims=True)
        - normed * jnp.mean(grad * normed, axis=-1, keepdims=True)
    )


def forward_kernel(
    core, x, w_own, w_far, seg, q_out, k_out, v_out, p_out, vec_out, keep, send, first_out, norm_out, scale_out,
    slope, w_other, wide, pair_scr, acts, sems,
):
    c = core[0]
    copies = []
    for i in range(3):
        lanes = pl.ds(1024 * i, 1024)
        copies.append(pltpu.make_async_copy(w_far.at[:, lanes], w_other.at[:, lanes], sems.at[i]))
        copies[i].start()
    sides = ((c, w_own), (1 - c, w_other))
    vec = w_own[:, VEC_LANE:BLOCK].astype(F32).T[:16]
    vec_out[...] = vec
    moved = dot(vec[8:16].astype(BF), regroup())
    for part in range(4):
        for q in range(4):
            vec_out[8 + q : 9 + q, 128 * part : 128 * (part + 1)] = moved[part : part + 1, 128 * q : 128 * (q + 1)]
    tokens = x[...]
    pair_scr[0] = tokens
    names = jnp.broadcast_to(seg[...].astype(F32), (ROW, ROW))
    gap = names - names.T
    same = jnp.concatenate([gap, gap], axis=0) == 0.0
    for half, w in sides:
        if w is w_other:
            copies[0].wait()
        product = dot(tokens, w[:, 0:O_LANE])
        q = (product[:, 0:HALF] + vec_out[0:1, half_lanes(half, HALF)]).astype(BF)
        k = product[:, HALF : 2 * HALF].astype(BF)
        v = (product[:, 2 * HALF : O_LANE] + vec_out[1:2, half_lanes(half, HALF)]).astype(BF)
        for target, value in ((q_out, q), (k_out, k), (v_out, v)):
            target[:, half_lanes(half, HALF)] = value
        for pair in range(2):
            cols = slice(128 * pair, 128 * pair + 128)
            scores = dot_t(by_head(q[:, cols]), k[:, cols]) * (HD ** (-0.5))
            scores = jnp.where(same, scores, MASKED_SCORE)
            expo = jnp.exp(scores - jnp.max(scores, axis=-1, keepdims=True))
            soft = expo / jnp.sum(expo, axis=-1, keepdims=True)
            p_out[2 * half + pair] = soft
            attended = dot(abreast(soft.astype(BF)), by_head(v[:, cols]))
            lanes = pl.ds(pl.multiple_of(HALF * half + 128 * pair, 128), 128)
            pair_scr[1, :, lanes] = attended.astype(BF)
    for half, w in sides:
        wide[:, half_lanes(half, HALF)] = dot(pair_scr[1], w[:, O_LANE:UP_LANE])
    normed, scale = norm_parts(tokens.astype(F32) + wide[...] + vec[2:3])
    norm_out[...] = normed
    scale_out[...] = scale
    first = normed * vec[4:5] + vec[5:6]
    first_out[...] = first
    first_low = first.astype(BF)
    root = math.sqrt(2.0 / math.pi)
    copies[1].wait()
    for half, w in sides:
        for k in range(2):
            bias = vec_out[pl.ds(8 + 2 * half + k, 1), :]
            u = dot(first_low, w[:, UP_LANE + D * k : UP_LANE + D * (k + 1)]) + bias
            square = u * u
            tanh = jnp.tanh(root * (u + 0.044715 * (square * u)))
            gate = 0.5 * (1.0 + tanh)
            cols = pl.ds(pl.multiple_of(1024 * half + D * k, D), D)
            slope[:, cols] = gate + 0.5 * u * (1.0 - tanh * tanh) * (root * (1.0 + 3 * 0.044715 * square))
            acts[:, cols] = (u * gate).astype(BF)
    for target, half in ((keep, c), (send, 1 - c)):
        target[:, X0:A0] = tokens
        target[:, A0:H0] = pair_scr[half]
        target[:, H0:Z0] = first_low
        target[:, Z0 : Z0 + 1024] = acts[:, half_lanes(half, 1024)]
        target[:, Z0 + 1024 : ACTS] = jnp.zeros((ROW, ACTS - Z0 - 1024), BF)
    copies[2].wait()


def backward_kernel(
    core, x, acts_own, acts_sent, first, vec_in, w_own, w_other, cot, slope, normed_in, scale_in, q_in, k_in, v_in, p_in,
    out, base, y_scr, keep, send, vg, wide, du_scr, df_scr, do_scr,
):
    c = core[0]
    sides = ((c, w_own), (1 - c, w_other))
    vec = vec_in[...]
    dq_scr, dk_scr, dv_scr, da_scr = (y_scr.at[i] for i in range(4))
    for half, w in sides:
        feed = jnp.zeros((ROW, HALF), F32)
        for group, acts in ((c, acts_own), (1 - c, acts_sent)):
            for k in range(2):
                lanes = pl.ds(pl.multiple_of(DOWN_LANE + 2 * HALF * group + HALF * k, HALF), HALF)
                feed = feed + dot(acts[:, Z0 + D * k : Z0 + D * (k + 1)], w[:, lanes])
        wide[:, half_lanes(half, HALF)] = feed
    residual = wide[...] + vec[3:4] + first[...] + x[...].astype(F32)
    normed, scale = norm_parts(residual)
    out[...] = (normed * vec[6:7] + vec[7:8]).astype(BF)
    grad = cot[...].astype(F32)
    vg[...] = jnp.zeros((16, D), F32)
    vg[6:7, :] = jnp.sum(grad * normed, axis=0, keepdims=True)
    vg[7:8, :] = jnp.sum(grad, axis=0, keepdims=True)
    grad2 = norm_back(grad, vec[6:7], normed, scale)
    df_scr[...] = grad2.astype(BF)
    vg[3:4, :] = jnp.sum(df_scr[...].astype(F32), axis=0, keepdims=True)
    for q in range(4):
        lane = DOWN_LANE + HALF * q
        dz = dot_t(df_scr[:, half_lanes(c, HALF)], w_own[:, lane : lane + HALF])
        dz = dz + dot_t(df_scr[:, half_lanes(1 - c, HALF)], w_other[:, lane : lane + HALF])
        du = (dz * slope[:, D * q : D * (q + 1)]).astype(BF)
        du_scr[:, D * q : D * (q + 1)] = du
        vg[8 + q : 9 + q, :] = jnp.sum(du.astype(F32), axis=0, keepdims=True)
    dfirst = grad2
    for half, w in sides:
        dfirst = dfirst + dot_t(du_scr[:, half_lanes(half, 1024)], w[:, UP_LANE:DOWN_LANE])
    normed1 = normed_in[...]
    vg[4:5, :] = jnp.sum(dfirst * normed1, axis=0, keepdims=True)
    vg[5:6, :] = jnp.sum(dfirst, axis=0, keepdims=True)
    dres = norm_back(dfirst, vec[4:5], normed1, scale_in[...])
    da_scr[...] = dres.astype(BF)
    vg[2:3, :] = jnp.sum(da_scr[...].astype(F32), axis=0, keepdims=True)
    dattended = jnp.zeros((ROW, D), F32)
    for half, w in sides:
        dattended = dattended + dot_t(da_scr[:, half_lanes(half, HALF)], w[:, O_LANE:UP_LANE])
    do_scr[...] = dattended.astype(BF)
    share = HD ** (-0.5)
    pairs = [slice(128 * pair, 128 * pair + 128) for pair in range(H // 2)]
    dos = [by_head(do_scr[:, cols]) for cols in pairs]
    dsofts = [dot_t(do, v_in[:, cols]) for do, cols in zip(dos, pairs)]
    dss = []
    for pair, dsoft in enumerate(dsofts):
        soft = p_in[pair]
        dss.append((soft * (dsoft - jnp.sum(soft * dsoft, axis=-1, keepdims=True))).astype(BF))
    for pair, cols in enumerate(pairs):
        ds = dss[pair]
        dq_scr[:, cols] = (dot(abreast(ds), by_head(k_in[:, cols])) * share).astype(BF)
        dk_scr[:, cols] = (dot_in(ds, by_head(q_in[:, cols])) * share).astype(BF)
        dv_scr[:, cols] = dot_in(p_in[pair].astype(BF), dos[pair]).astype(BF)
    vg[0:1, :] = jnp.sum(dq_scr[...].astype(F32), axis=0, keepdims=True)
    vg[1:2, :] = jnp.sum(dv_scr[...].astype(F32), axis=0, keepdims=True)
    for target, half in ((keep, c), (send, 1 - c)):
        target[:, 0:D] = y_scr[half]
        target[:, D : 2 * D] = y_scr[2 + half]
        target[:, DU0:DF0] = du_scr[:, half_lanes(half, 1024)]
        target[:, DF0:GRADS] = df_scr[...]
    base[...] = grad2 + dres


def input_kernel(core, base, grads, w_own, w_other, out):
    total = base[...]
    for half, w in ((core[0], w_own), (1 - core[0], w_other)):
        for i in range(3):
            total = total + dot_t(grads[i, :, half_lanes(half, HALF)], w[:, HALF * i : HALF * (i + 1)])
    out[...] = total.astype(BF)


def weights_kernel(acts, acts_other, keep, got, vg, vg_other, out, vec):
    def both(one, two, first, last):
        return jnp.concatenate([one[:, first:last], two[:, first:last]], axis=0)

    out[:, UP_LANE:DOWN_LANE] = dot_in(both(acts, acts_other, H0, Z0), both(keep, got, DU0, DF0)).astype(BF)
    down = both(keep, got, DF0, GRADS)
    for k in range(2):
        lane = DOWN_LANE + D * k
        units = both(acts, acts_other, Z0 + D * k, Z0 + D * (k + 1))
        out[:, lane : lane + D] = dot_in(units, down).astype(BF)
    for k in range(2):
        left = both(acts, acts_other, D * k, D * (k + 1))
        out[:, D * k : D * (k + 1)] = dot_in(left, both(keep, got, D * k, D * (k + 1))).astype(BF)
    total = vg[...] + vg_other[...]
    vec[...] = jnp.zeros((128, D), F32)
    vec[0:8, :] = total[0:8]
    for part in range(4):
        for q in range(4):
            vec[8 + part : 9 + part, 128 * q : 128 * (q + 1)] = total[8 + q : 9 + q, 128 * part : 128 * (part + 1)]
    vec[8:16, :] = dot_t(vec[8:16, :].astype(BF), regroup())
    out[:, VEC_LANE:BLOCK] = vec[...].T.astype(BF)


def add_up(ref):
    total = ref[0].astype(F32)
    for i in range(1, 64):
        total = total + ref[i].astype(F32)
    return total


def split3(value):
    one = value.astype(BF)
    rest = value - one.astype(F32)
    two = rest.astype(BF)
    three = (rest - two.astype(F32)).astype(BF)
    return one, two, three


def reduce_kernel(got, grads, pay):
    grads[...] = add_up(got)
    own, vec = grads[:, 0:VEC_LANE], grads[:, VEC_LANE:BLOCK]
    square = jnp.sum(own * own) + 0.5 * jnp.sum(vec * vec)
    row = lax.broadcasted_iota(jnp.int32, (8, 128), 0)
    lane = lax.broadcasted_iota(jnp.int32, (8, 128), 1)
    full = jnp.full((8, 128), square, F32)
    one, two, three = split3(full)
    note = jnp.where(lane == 0, one.astype(F32), jnp.where(lane == 1, two.astype(F32), three.astype(F32)))
    note = jnp.where((row == 0) & (lane < 3), note, 0.0).astype(BF)
    rows = role_lanes(grads[:, 0:VEC_LANE].astype(BF), note)
    for i in range(64):
        pay[i] = rows[i % 4]


def halves(value):
    high = value.astype(BF)
    return high, (value - high.astype(F32)).astype(BF)


def fine(a, b):
    ah, al = a
    bh, bl = b
    return dot(jnp.concatenate([ah, ah, al], axis=1), jnp.concatenate([bh, bl, bh], axis=0))


TALL = 3 * HALF + 8


def near_kernel(far, near, sem):
    copy = pltpu.make_async_copy(far, near, sem)
    copy.start()
    copy.wait()


def note_kernel(got, note):
    note[...] = jnp.full((8, 128), jnp.sum(got[:, 1024:1152].astype(F32)), F32)


def gram_kernel(role_ref, got, mom, note, note_other, matrix, gram, clip_out, factor_out):
    role = role_ref[0]
    clip = jnp.sqrt(note[...] + note_other[...])
    factors = CLIP_LIMIT / jnp.maximum(clip, CLIP_LIMIT)
    clip_out[...] = clip[0:1, 0:1]
    factor_out[...] = factors
    factor = factors[0:1, 0:1]

    def make(k):
        cols = slice(D * k, D * (k + 1))
        value = MOMENTUM_DECAY * mom[:, cols].astype(F32) + factor * got[:, cols].astype(F32)
        value = value.astype(BF)
        matrix[k] = value
        value = value.astype(F32)
        return jnp.sum(value * value)

    def finish(product, parts, square):
        for i, (a, b) in enumerate(((0, 0), (0, 1), (1, 1))):
            total = product(a, b, 0)
            for k in range(1, parts):
                total = total + product(a, b, k)
            gram[HALF * i : HALF * (i + 1), :] = total
        gram[3 * HALF : TALL, :] = jnp.full((8, HALF), square, F32)

    def inner(a, b, k):
        return dot_in(matrix[k, :, HALF * a : HALF * (a + 1)], matrix[k, :, HALF * b : HALF * (b + 1)])

    def outer(a, b, k):
        return dot_t(matrix[k, HALF * a : HALF * (a + 1), :], matrix[k, HALF * b : HALF * (b + 1), :])

    @pl.when(role < 2)
    def _():
        square = make(0)
        finish(inner, 1, square)

    @pl.when(role == 2)
    def _():
        square = make(0) + make(1)
        finish(outer, 2, square)

    @pl.when(role == 3)
    def _():
        square = make(0) + make(1)
        finish(inner, 2, square)


def thin(rows, matrix):
    high, low = halves(rows)
    both = dot(jnp.concatenate([high, low], axis=0), matrix[0])
    return both[0 : rows.shape[0]] + (both[rows.shape[0] :] + dot(high, matrix[1]))


def newton_kernel(role_ref, plane_ref, matrix, gram_own, gram_other, out, gram, rows_scr):
    role, plane = role_ref[0], plane_ref[0]
    chips = pl.ds(pl.multiple_of(plane * 32, 32), 32)

    def scaled(total):
        size = jnp.sqrt(total[3 * HALF : 3 * HALF + 1, 0:1]) + 1e-07
        inverse = 1.0 / size
        total = total[0 : 3 * HALF] * (inverse * inverse)
        gram[0:HALF, 0:HALF] = total[0:HALF]
        gram[0:HALF, HALF:D] = total[HALF:D]
        gram[HALF:D, 0:HALF] = total[HALF:D].T
        gram[HALF:D, HALF:D] = total[D : 3 * HALF]
        return inverse

    def rows_of(k):
        return matrix[k, chips, :].astype(F32)

    @pl.when(role < 2)
    def _():
        inverse = scaled(gram_own[...])
        rows_scr[0:32, :] = rows_of(0) * inverse
        rows_scr[32:64, :] = jnp.zeros((32, D), F32)

    @pl.when(role == 2)
    def _():
        inverse = scaled(gram_own[...] + gram_other[...])
        here = lax.broadcasted_iota(jnp.int32, (32, D), 0) + 32 * plane
        there = lax.broadcasted_iota(jnp.int32, (32, D), 1)
        rows_scr[0:32, :] = jnp.where(here == there, 1.0, 0.0) * inverse
        rows_scr[32:64, :] = jnp.zeros((32, D), F32)

    @pl.when(role == 3)
    def _():
        inverse = scaled(gram_own[...] + gram_other[...])
        for k in range(2):
            rows_scr[32 * k : 32 * (k + 1), :] = rows_of(k) * inverse

    diagonal = (
        lax.broadcasted_iota(jnp.int32, (D, D), 0) == lax.broadcasted_iota(jnp.int32, (D, D), 1)
    )

    def polynomial(square):
        poly = NEWTON_SECOND * gram[...] + NEWTON_THIRD * square
        return jnp.where(diagonal, poly + NEWTON_FIRST, poly)

    def turn(_):
        own = halves(gram[...])
        poly = halves(polynomial(dot(own[0], own[0])))
        pairs = zip(halves(fine(poly, own)), halves(rows_scr[...]))
        both = fine(tuple(jnp.concatenate(pair, axis=0) for pair in pairs), poly)
        gram[...] = both[0:D]
        rows_scr[...] = both[D:]

    pl.loop(0, NS_ITERS - 2)(turn)
    own = halves(gram[...])
    poly = halves(polynomial(fine(own, own)))
    rows = thin(rows_scr[...], poly)

    def through(value):
        return thin(thin(thin(value, poly), poly), own)

    once = through(rows)
    twice = through(once)
    rows_scr[...] = NEWTON_FIRST * rows + NEWTON_SECOND * once + NEWTON_THIRD * twice

    def send(k, value):
        value = value.astype(BF).reshape(4, 8, D)
        out[:, 0, :, D * k : D * (k + 1)] = value
        out[:, 1, :, D * k : D * (k + 1)] = value

    @pl.when(role == 2)
    def _():
        high, low = halves(rows_scr[0:32, :])
        for k in range(2):
            send(k, dot(high, matrix[k]) + dot(low, matrix[k]))

    @pl.when(role != 2)
    def _():
        for k in range(2):
            send(k, rows_scr[32 * k : 32 * (k + 1), :])


def rows4(is_left, value):
    return jnp.where(is_left, value[0:4], value[4:8])


def natural(ups):
    parts = [
        jnp.concatenate([ups[:, D * q + 128 * part : D * q + 128 * (part + 1)] for q in range(4)], axis=1)
        for part in range(4)
    ]
    return dot_t(jnp.concatenate(parts, axis=0).astype(BF), regroup())


def momenta_kernel(
    core, grads, grads_other, factors, vec, attn_m, up_m, down_m, vec_m, vec_s,
    attn_mom, up_mom, down_mom, vec_mom, vec_sec, vec_new, vec_copy, ups, downs,
):
    is_left = core[0] == 0
    factor = factors[0:1, 0:1]

    def both(first, last):
        mine, other = grads[:, first:last], grads_other[:, first:last]
        left = jnp.where(is_left, mine, other)
        right = jnp.where(is_left, other, mine)
        return rows4(is_left, left), rows4(is_left, right)

    pairs = [both(D * k, D * (k + 1)) for k in range(2)]
    for m in range(4):
        attn_mom[m] = MOMENTUM_DECAY * attn_m[m] + factor * pairs[m // 2][m % 2]
    high, low = halves(jnp.concatenate(both(UP_LANE, DOWN_LANE), axis=1))
    ups[0:4, :] = high.astype(F32)
    ups[4:8, :] = low.astype(F32)
    moved = natural(ups)
    for part in range(4):
        cols = slice(D * part, D * (part + 1))
        grad = moved[8 * part : 8 * part + 4] + moved[8 * part + 4 : 8 * part + 8]
        up_mom[:, cols] = MOMENTUM_DECAY * up_m[:, cols] + factor * grad
    sides = both(DOWN_LANE, VEC_LANE)
    for q in range(4):
        grad = sides[q // 2][:, D * (q % 2) : D * (q % 2 + 1)]
        for i in range(4):
            downs[4 * i + q : 4 * i + q + 1, :] = grad[i : i + 1]
    down_mom[...] = MOMENTUM_DECAY * down_m[...] + factor * downs[...]
    clipped = factor * rows4(is_left, grads[:, VEC_LANE:BLOCK])[:, 0:12]
    first = BETA_FIRST * vec_m[...] + (1.0 - BETA_FIRST) * clipped
    second = BETA_SECOND * vec_s[...] + (1.0 - BETA_SECOND) * clipped * clipped
    vec_mom[...] = first
    vec_sec[...] = second
    first_hat = first / (1.0 - BETA_FIRST**STEP)
    second_hat = second / (1.0 - BETA_SECOND**STEP)
    new = vec[...] - RATE_VECTOR * first_hat / (jnp.sqrt(second_hat) + ADAM_EPSILON)
    vec_new[...] = new
    vec_copy[...] = new.astype(BF)


def update_kernel(
    core, got, attn, up, down, attn_new, up_new, down_new, attn_copy, up_copy, down_copy, ups, downs
):
    is_left = core[0] == 0
    keep_share = 1.0 - RATE_MATRIX * DECAY_MATRIX
    for m in range(4):
        new = attn[m] * keep_share - RATE_MATRIX * rows4(is_left, got[m, :, 0:512].astype(F32))
        attn_new[m] = new
        attn_copy[m] = new.astype(BF)
    ups[0:4, :] = rows4(is_left, jnp.concatenate([got[4].astype(F32), got[5].astype(F32)], axis=1))
    ups[4:8, :] = jnp.zeros((4, FF), F32)
    rate = RATE_MATRIX * math.sqrt(max(1.0, FF / D))
    moved = natural(ups)
    for part in range(4):
        cols = slice(D * part, D * (part + 1))
        up_new[:, cols] = up[:, cols] * keep_share - rate * moved[8 * part : 8 * part + 4]
    up_copy[...] = up_new[...].astype(BF)
    rate = RATE_MATRIX * math.sqrt(max(1.0, D / FF))
    for q in range(4):
        step = rows4(is_left, got[6 + q // 2, :, D * (q % 2) : D * (q % 2 + 1)].astype(F32))
        for i in range(4):
            downs[4 * i + q : 4 * i + q + 1, :] = step[i : i + 1]
    down_new[...] = down[...] * keep_share - rate * downs[...]
    down_copy[...] = down_new[...].astype(BF)


def swap(value):
    return lax.ppermute(value, "c", [(0, 1), (1, 0)])


def to_chips(value):
    return lax.all_to_all(value, CHIPS, 0, 0, tiled=True)


def body(
    block_input, cotangent, segment_ids, attn_master, up_master, down_master, vec_master,
    attn_moment, up_moment, down_moment, vec_moment, vec_second,
):
    c = lax.axis_index("c")
    core = c.reshape(1).astype(jnp.int32)
    role = lax.axis_index("y").reshape(1).astype(jnp.int32)
    plane = (lax.axis_index("x") * 4 + lax.axis_index("z")).reshape(1).astype(jnp.int32)
    core, role, plane = lax.optimization_barrier((core, role, plane))

    keep, send = call(
        pack_kernel,
        [((8, BLOCK), BF)] * 2,
        [core, attn_master, up_master, down_master, vec_master.T, attn_moment, up_moment, down_moment],
        scratch=[
            pltpu.VMEM((4, 4, D), F32), pltpu.VMEM((4, FF), F32), pltpu.VMEM((16, D), F32), pltpu.VMEM((4, 12), F32),
            pltpu.VMEM((4, 4, D), F32), pltpu.VMEM((4, FF), F32), pltpu.VMEM((16, D), F32),
            pltpu.VMEM((8, 3 * FF), F32), pltpu.VMEM((8, BLOCK), F32), pltpu.VMEM((32, D), F32),
            pltpu.SemaphoreType.DMA((7,)),
        ],
        smem=(0,),
        far=range(1, 8),
    )
    message, message_mom = call(
        spread_kernel, [((64, 8, BLOCK), BF), ((64, 8, 1024), BF)], [core, keep, swap(send)], smem=(0,)
    )
    own = to_chips(message)
    own, message_mom = lax.optimization_barrier((own, message_mom))
    other = swap(own)
    mom = to_chips(message_mom).reshape(D, 1024)
    own, other = own.reshape(D, BLOCK), other.reshape(D, BLOCK)
    q, k, v, soft, vec, acts_own, acts_sent, first, normed, scale, slope, other = call(
        forward_kernel,
        [((ROW, D), BF)] * 3
        + [((H // 2, 2 * ROW, ROW), F32), ((16, D), F32), ((ROW, ACTS), BF), ((ROW, ACTS), BF)]
        + [((ROW, D), F32), ((ROW, D), F32), ((ROW, 1), F32), ((ROW, FF), F32), ((D, 3072), BF)],
        [core, block_input, own, other, segment_ids],
        scratch=[
            pltpu.VMEM((ROW, D), F32), pltpu.VMEM((2, ROW, D), BF), pltpu.VMEM((ROW, FF), BF),
            pltpu.SemaphoreType.DMA((3,)),
        ],
        smem=(0,),
        args=(1, 4),
        far=(3,),
        flops=8 * 2 * ROW * D * D,
    )
    acts_other = swap(acts_sent)
    layer_out, base, ygrads, keep, send, vg = call(
        backward_kernel,
        [((ROW, D), BF), ((ROW, D), F32), ((4, ROW, D), BF), ((ROW, GRADS), BF), ((ROW, GRADS), BF), ((16, D), F32)],
        [
            core, block_input, acts_own, acts_sent, first, vec, own, other, cotangent, slope, normed, scale,
            q, k, v, soft,
        ],
        scratch=[
            pltpu.VMEM((ROW, D), F32), pltpu.VMEM((ROW, FF), BF), pltpu.VMEM((ROW, D), BF), pltpu.VMEM((ROW, D), BF),
        ],
        smem=(0,),
        args=(1, 8),
        results=(0,),
        flops=18 * 2 * ROW * D * D,
    )
    got, vg_other = swap(send), swap(vg)
    (input_grad,) = call(
        input_kernel,
        [((ROW, D), BF)],
        [core, base, ygrads, own, other],
        smem=(0,),
        results=(0,),
        flops=3 * 2 * ROW * D * D,
    )
    got, input_grad = lax.optimization_barrier((got, input_grad))
    (weights,) = call(
        weights_kernel,
        [((D, BLOCK), BF)],
        [acts_own, acts_other, keep, got, vg, vg_other],
        scratch=[pltpu.VMEM((128, D), F32)],
        flops=2 * 256 * 512 * 3072,
    )
    weights, mom = lax.optimization_barrier((weights, mom))
    weights = to_chips(weights.reshape(64, 8, BLOCK))
    grads, pay = call(reduce_kernel, [((8, BLOCK), F32), ((64, 8, 1152), BF)], [weights])
    pay = to_chips(pay)
    pay, mom, grads = lax.optimization_barrier((pay, mom, grads))
    (note,) = call(note_kernel, [((8, 128), F32)], [pay.reshape(D, 1152)])
    note_other, grads_other = swap(note), swap(grads)
    (mom,) = call(near_kernel, [((D, 1024), BF)], [mom], scratch=[pltpu.SemaphoreType.DMA], far=(0,))
    note_other, grads_other, mom = lax.optimization_barrier((note_other, grads_other, mom))
    matrix, gram, clip_norm, factors = call(
        gram_kernel,
        [((2, D, D), BF), ((TALL, HALF), F32), ((1, 1), F32), ((8, 128), F32)],
        [role, pay.reshape(D, 1152), mom, note, note_other],
        smem=(0,),
        results=(2,),
        flops=2 * 2 * D * D * D,
    )
    gram_other = swap(gram)
    *moms, vec_mom, vec_sec, vec_new, vec_copy = call(
        momenta_kernel,
        [((4, 4, D), F32), ((4, FF), F32), ((16, D), F32)] + [((4, 12), F32)] * 3 + [((4, 12), BF)],
        [
            core, grads, grads_other, factors, vec_master.T, attn_moment, up_moment, down_moment,
            vec_moment.T, vec_second.T,
        ],
        scratch=[pltpu.VMEM((8, FF), F32), pltpu.VMEM((16, D), F32)],
        smem=(0,),
        args=range(4, 10),
        results=range(7),
    )
    gram_other, *moms = lax.optimization_barrier((gram_other, *moms))
    vecs = [t.T for t in (vec_mom, vec_sec, vec_new, vec_copy)]
    (orth,) = call(
        newton_kernel,
        [((4, 2, 8, 1024), BF)],
        [role, plane, matrix, gram, gram_other],
        scratch=[pltpu.VMEM((D, D), F32), pltpu.VMEM((64, D), F32)],
        smem=(0, 1),
        flops=14 * 3 * 2 * D * D * D,
    )
    orth = orth.reshape(8, 8, 1024)
    orth = lax.all_to_all(orth, ("y", "c"), 0, 0, tiled=True)
    news = call(
        update_kernel,
        [((4, 4, D), F32), ((4, FF), F32), ((16, D), F32), ((4, 4, D), BF), ((4, FF), BF), ((16, D), BF)],
        [core, orth, attn_master, up_master, down_master],
        scratch=[pltpu.VMEM((8, FF), F32), pltpu.VMEM((16, D), F32)],
        smem=(0,),
        args=range(2, 5),
        results=range(6),
    )
    return (layer_out, input_grad, clip_norm[0, 0], *moms, *news, *vecs)


def solution(mesh):
    grid = Mesh(mesh.devices.reshape(4, 4, 4, 2), ("x", "z", "y", "c"))
    row, mat, vec = P(ALL, None), P(None, ALL, None), P(None, ALL)
    return jax.shard_map(
        body,
        mesh=grid,
        in_specs=(row, row, row, mat, row, row, vec, mat, row, row, vec, vec),
        out_specs=(row, row, P(), mat, row, row, mat, row, row, mat, row, row, vec, vec, vec, vec),
        check_vma=False,
    )
```

profile of v0, /device:TPU:1, one launch (start us, length us, event | category | flops | bytes accessed | tf_op | source)
XLA Modules:
  0.0 180.8 jit_solution(4108496517031054802)
XLA Ops:
  0.7 1.2 shard_map.243
  1.8 1.5 collective-permute-start
  3.3 0.9 collective-permute-done.got
  4.2 0.3 shard_map.244
  4.5 0.0 copy-start
  4.6 0.0 copy-start.1
  4.6 0.0 copy-start.12
  4.6 51.8 %all_to_all.25 = bf16[64,8,3200]{2,1,0:T(8,128)(2,1)S(1)} all-to-all(bf16[64,8,3200]{2,1,0:T(8,128)(2,1)S(1)} %get-tuple-element.79), channel_id=1, replica_groups=mesh['x'=4,'z'=4,'y'=4,'c'=2] {'x','z','y'}, dimensions={0} | all-to-all | bytes 6553600 | tf_op jit(solution)/shard_map/all_to_all | solution.py:634
  56.4 0.0 copy-done
  56.4 2.9 %collective-permute-start.1 = (bf16[64,8,3200]{2,1,0:T(8,128)(2,1)S(1)}, bf16[64,8,3200]{2,1,0:T(8,128)(2,1)}, u32[]{:S(2)}, u32[]{:S(2)}) collective-permute-start(bf16[64,8,3200]{2,1,0:T(8,128)(2,1)S(1)} %all_to_all.25), channel_id=1, source_target_pairs={{0,1},{1,0},{2,3},{3,2},{4,5},{5,4},{6,7},{7,6},{8,9},{9,8},{10,11... | collective-permute-start | bytes 9830408 | tf_op jit(solution)/shard_map/ppermute | solution.py:630
  59.2 5.5 %all-to-all-start.1 = ((bf16[64,8,1024]{2,1,0:T(8,128)(2,1)}), bf16[64,8,1024]{2,1,0:T(8,128)(2,1)}, u32[]{:S(2)}, u32[]{:S(2)}) async-start(bf16[64,8,1024]{2,1,0:T(8,128)(2,1)} %copy-done), calls=%async_computation.1 | async-start | bytes 2097152 | tf_op jit(solution)/shard_map/all_to_all | solution.py:634
  64.8 0.1 collective-permute-done.1
  64.8 0.0 copy-done.1
  64.8 0.0 copy-done.12
  64.8 0.0 copy-start.2
  64.8 4.4 %shard_map.245 = (bf16[128,512]{1,0:T(8,128)(2,1)S(1)}, bf16[128,512]{1,0:T(8,128)(2,1)S(1)}, bf16[128,512]{1,0:T(8,128)(2,1)S(1)}, f32[4,256,128]{2,1,0:T(8,128...) custom-call(s32[1]{0:T(128)} %bitcast.core, ...), custom_call_target="tpu_custom_call" | custom-call | flops 536870912 | bytes 6685188 | tf_op jit(solution)/shard_map/pallas_call | solution.py:55
  69.2 0.5 collective-permute-start.3
  69.7 0.0 copy-done.2
  69.7 3.9 %shard_map.246 = (bf16[128,512]{1,0:T(8,128)(2,1)}, f32[128,512]{1,0:T(8,128)S(1)}, bf16[4,128,512]{2,1,0:T(8,128)(2,1)S(1)}, bf16[128,2560]{1,0:T(8,128)(2,1)S(...) custom-call(s32[1]{0:T(128)} %bitcast.core, bf16[128,512]{1,0:T(8,128)(2,1)S(1)} %copy-done.1, ...), custom_call_target="tpu_custom_call" | custom-call | flops 1207959552 | bytes 10912260 | tf_op jit(solution)/shard_map/pallas_call | solution.py:55
  73.6 0.1 collective-permute-start.2
  73.7 0.4 collective-permute-start.4
  74.1 1.3 shard_map.247
  75.4 0.3 collective-permute-done.2.got
  75.7 0.0 collective-permute-done.4.vg_other
  75.7 0.0 collective-permute-done.3.acts_other
  75.8 1.2 shard_map.248
  76.9 5.2 %all-to-all-done.1 = bf16[64,8,1024]{2,1,0:T(8,128)(2,1)} async-done(((bf16[64,8,1024]{2,1,0:T(8,128)(2,1)}), bf16[64,8,1024]{2,1,0:T(8,128)(2,1)}, u32[]{:S(2)}, u32[]{:S(2)}) %all-to-all-start.1) | async-done | bytes 1048608 | tf_op jit(solution)/shard_map/all_to_all | solution.py:634
  82.1 45.0 %all_to_all.26.got = bf16[64,8,3200]{2,1,0:T(8,128)(2,1)S(1)} all-to-all(bf16[64,8,3200]{2,1,0:T(8,128)(2,1)S(1)} %bitcast.20), channel_id=1, replica_groups=mesh['x'=4,'z'=4,'y'=4,'c'=2] {'x','z','y'}, dimensions={0} | all-to-all | bytes 6553600 | tf_op jit(solution)/shard_map/all_to_all | solution.py:634
  127.1 0.6 shard_map.249
  127.7 24.7 %all_to_all.27 = bf16[64,8,1152]{2,1,0:T(8,128)(2,1)S(1)} all-to-all(bf16[64,8,1152]{2,1,0:T(8,128)(2,1)S(1)} %get-tuple-element.105), channel_id=1, replica_groups=mesh['x'=4,'z'=4,'y'=4,'c'=2] {'x','z','y'}, dimensions={0} | all-to-all | bytes 2359296 | tf_op jit(solution)/shard_map/all_to_all | solution.py:634
  152.4 0.0 copy-start.3
  152.4 0.0 copy-start.4
  152.4 0.0 copy-start.5
  152.4 0.0 copy-start.9
  152.4 0.0 copy-start.10
  152.4 0.0 copy-start.11
  152.5 3.8 %collective-permute-start.6 = (f32[8,3200]{1,0:T(8,128)S(1)}, f32[8,3200]{1,0:T(8,128)S(1)}, u32[]{:S(2)}, u32[]{:S(2)}) collective-permute-start(f32[8,3200]{1,0:T(8,128)S(1)} %get-tuple-element.109.grads), channel_id=1, source_target_pairs={{0,1},{1,0},{2,3},{3,2},{4,5},{5,4},{6,7},{7,6},{8,9},{9,8},{10,11... | collective-permute-start | bytes 307208 | tf_op jit(solution)/shard_map/ppermute | solution.py:630
  156.3 0.2 shard_map.250.note
  156.5 0.1 collective-permute-start.5
  156.6 1.2 shard_map.251.mom
  157.8 0.0 collective-permute-done.5.note_other
  157.8 0.0 collective-permute-done.6.grads_other
  157.8 1.2 shard_map.252
  159.0 0.5 collective-permute-start.7
  159.5 0.0 copy-done.3
  159.5 0.0 copy-done.4
  159.5 0.0 copy-done.5
  159.5 0.0 copy-done.9
  159.5 0.0 copy-done.10
  159.5 0.0 copy-done.11
  159.5 0.9 shard_map.253
  160.5 0.9 collective-permute-done.7.gram_other
  161.4 0.0 copy-start.6
  161.4 0.0 copy-start.7
  161.4 0.0 copy-start.8
  161.4 9.5 %shard_map.254 = bf16[4,2,8,1024]{3,2,1,0:T(8,128)(2,1)S(1)} custom-call(s32[1]{0:T(128)} %bitcast.1.role_ref, s32[1]{0:T(128)} %bitcast.2.plane_ref, bf16[2,512,512]{2,1,0:T(8,128)(2,1)S(1)} %get-tuple-element.124.matrix, f32[776,256]{1,0:T(8,128)S(1)} %get-tuple-element.114.gram_own, f32[776,256]{1,0:T(8,128)S(1)} %collective-permute-done.7.gram_other), custom_call_target="tpu_custom_call" | custom-call | flops 11274289152 | bytes 2637832 | tf_op jit(solution)/shard_map/pallas_call | solution.py:55
  170.9 8.9 %all_to_all.28.got = bf16[8,8,1024]{2,1,0:T(8,128)(2,1)S(1)} all-to-all(bf16[8,8,1024]{2,1,0:T(8,128)(2,1)S(1)} %bitcast.23), channel_id=1, replica_groups=mesh['x'=4,'z'=4,'y'=4,'c'=2] {'y','c'}, dimensions={0} | all-to-all | bytes 262144 | tf_op jit(solution)/shard_map/all_to_all | solution.py:757
  179.8 0.0 copy-done.6
  179.8 0.0 copy-done.7
  179.8 0.0 copy-done.8
  179.8 0.9 shard_map.255
Async XLA Ops:
  1.8 2.4 %collective-permute-start = (bf16[8,3200]{1,0:T(8,128)(2,1)S(1)}, bf16[8,3200]{1,0:T(8,128)(2,1)S(1)}, u32[]{:S(2)}, u32[]{:S(2)}) collective-permute-start(bf16[8,3200]{1,0:T(8,128)(2,1)S(1)} %get-tuple-element.78), channel_id=1, source_target_pairs={{0,1},{1,0},{2,3},{3,2},{4,5},{5,4},{6,7},{7,6},{8,9},{9,8},{10,11... | collective-permute-start | bytes 153608 | tf_op jit(solution)/shard_map/ppermute | solution.py:630
  4.5 51.8 %copy-start = (bf16[64,8,1024]{2,1,0:T(8,128)(2,1)}, bf16[64,8,1024]{2,1,0:T(8,128)(2,1)S(1)}, u32[]{:S(2)}) copy-start(bf16[64,8,1024]{2,1,0:T(8,128)(2,1)S(1)} %get-tuple-element.103) | copy-start | bytes 3145732
  4.6 60.3 %copy-start.1 = (bf16[128,512]{1,0:T(8,128)(2,1)S(1)}, bf16[128,512]{1,0:T(8,128)(2,1)}, u32[]{:S(2)}) copy-start(bf16[128,512]{1,0:T(8,128)(2,1)} %x.3) | copy-start | bytes 393220
  4.6 60.3 %copy-start.12 = (s32[1,128]{1,0:T(1,128)S(1)}, s32[1,128]{1,0:T(1,128)}, u32[]{:S(2)}) copy-start(s32[1,128]{1,0:T(1,128)} %seg.1) | copy-start | bytes 1540
  56.4 8.5 %collective-permute-start.1 = (bf16[64,8,3200]{2,1,0:T(8,128)(2,1)S(1)}, bf16[64,8,3200]{2,1,0:T(8,128)(2,1)}, u32[]{:S(2)}, u32[]{:S(2)}) collective-permute-start(bf16[64,8,3200]{2,1,0:T(8,128)(2,1)S(1)} %all_to_all.25), channel_id=1, source_target_pairs={{0,1},{1,0},{2,3},{3,2},{4,5},{5,4},{6,7},{7,6},{8,9},{9,8},{10,11... | collective-permute-start | bytes 9830408 | tf_op jit(solution)/shard_map/ppermute | solution.py:630
  59.2 22.9 %all-to-all-start.1 = ((bf16[64,8,1024]{2,1,0:T(8,128)(2,1)}), bf16[64,8,1024]{2,1,0:T(8,128)(2,1)}, u32[]{:S(2)}, u32[]{:S(2)}) async-start(bf16[64,8,1024]{2,1,0:T(8,128)(2,1)} %copy-done), calls=%async_computation.1 | async-start | bytes 2097152 | tf_op jit(solution)/shard_map/all_to_all | solution.py:634
  64.8 4.9 %copy-start.2 = (bf16[128,512]{1,0:T(8,128)(2,1)S(1)}, bf16[128,512]{1,0:T(8,128)(2,1)}, u32[]{:S(2)}) copy-start(bf16[128,512]{1,0:T(8,128)(2,1)} %cot.1) | copy-start | bytes 393220
  69.2 6.5 %collective-permute-start.3 = (bf16[128,3328]{1,0:T(8,128)(2,1)S(1)}, bf16[128,3328]{1,0:T(8,128)(2,1)S(1)}, u32[]{:S(2)}, u32[]{:S(2)}) collective-permute-start(bf16[128,3328]{1,0:T(8,128)(2,1)S(1)} %get-tuple-element.83.acts_sent), channel_id=1, source_target_pairs={{0,1},{1,0},{2,3},{3,2},{4,5},{5,4},{6,7},{7,6},{8,9},{9,8},{10,11... | collective-permute-start | bytes 2555912 | tf_op jit(solution)/shard_map/ppermute | solution.py:630
  73.6 2.1 %collective-permute-start.2 = (bf16[128,2560]{1,0:T(8,128)(2,1)S(1)}, bf16[128,2560]{1,0:T(8,128)(2,1)S(1)}, u32[]{:S(2)}, u32[]{:S(2)}) collective-permute-start(bf16[128,2560]{1,0:T(8,128)(2,1)S(1)} %get-tuple-element.95), channel_id=1, source_target_pairs={{0,1},{1,0},{2,3},{3,2},{4,5},{5,4},{6,7},{7,6},{8,9},{9,8},{10,11... | collective-permute-start | bytes 1966088 | tf_op jit(solution)/shard_map/ppermute | solution.py:630
  73.7 2.0 %collective-permute-start.4 = (f32[16,512]{1,0:T(8,128)S(1)}, f32[16,512]{1,0:T(8,128)S(1)}, u32[]{:S(2)}, u32[]{:S(2)}) collective-permute-start(f32[16,512]{1,0:T(8,128)S(1)} %get-tuple-element.102.vg), channel_id=1, source_target_pairs={{0,1},{1,0},{2,3},{3,2},{4,5},{5,4},{6,7},{7,6},{8,9},{9,8},{10,11... | collective-permute-start | bytes 98312 | tf_op jit(solution)/shard_map/ppermute | solution.py:630
  152.4 7.1 %copy-start.3 = (f32[4,4,512]{2,1,0:T(4,128)S(1)}, f32[4,4,512]{2,1,0:T(4,128)}, u32[]{:S(2)}) copy-start(f32[4,4,512]{2,1,0:T(4,128)} %attn_m.3) | copy-start | bytes 98308
  152.4 7.1 %copy-start.4 = (f32[4,2048]{1,0:T(4,128)S(1)}, f32[4,2048]{1,0:T(4,128)}, u32[]{:S(2)}) copy-start(f32[4,2048]{1,0:T(4,128)} %up_m.3) | copy-start | bytes 98308
  152.4 7.1 %copy-start.5 = (f32[16,512]{1,0:T(8,128)S(1)}, f32[16,512]{1,0:T(8,128)}, u32[]{:S(2)}) copy-start(f32[16,512]{1,0:T(8,128)} %down_m.3) | copy-start | bytes 98308
  152.4 7.1 %copy-start.9 = (f32[12,4]{0,1:T(4,128)S(1)}, f32[12,4]{0,1:T(4,128)}, u32[]{:S(2)}) copy-start(f32[12,4]{0,1:T(4,128)} %param.18) | copy-start | bytes 580
  152.4 7.1 %copy-start.10 = (f32[12,4]{0,1:T(4,128)S(1)}, f32[12,4]{0,1:T(4,128)}, u32[]{:S(2)}) copy-start(f32[12,4]{0,1:T(4,128)} %param.22) | copy-start | bytes 580
  152.4 7.1 %copy-start.11 = (f32[12,4]{0,1:T(4,128)S(1)}, f32[12,4]{0,1:T(4,128)}, u32[]{:S(2)}) copy-start(f32[12,4]{0,1:T(4,128)} %param.23) | copy-start | bytes 580
  152.5 5.4 %collective-permute-start.6 = (f32[8,3200]{1,0:T(8,128)S(1)}, f32[8,3200]{1,0:T(8,128)S(1)}, u32[]{:S(2)}, u32[]{:S(2)}) collective-permute-start(f32[8,3200]{1,0:T(8,128)S(1)} %get-tuple-element.109.grads), channel_id=1, source_target_pairs={{0,1},{1,0},{2,3},{3,2},{4,5},{5,4},{6,7},{7,6},{8,9},{9,8},{10,11... | collective-permute-start | bytes 307208 | tf_op jit(solution)/shard_map/ppermute | solution.py:630
  156.5 1.3 collective-permute-start.5
  159.0 2.4 %collective-permute-start.7 = (f32[776,256]{1,0:T(8,128)S(1)}, f32[776,256]{1,0:T(8,128)S(1)}, u32[]{:S(2)}, u32[]{:S(2)}) collective-permute-start(f32[776,256]{1,0:T(8,128)S(1)} %get-tuple-element.114.gram_own), channel_id=1, source_target_pairs={{0,1},{1,0},{2,3},{3,2},{4,5},{5,4},{6,7},{7,6},{8,9},{9,8},{10,11... | collective-permute-start | bytes 2383880 | tf_op jit(solution)/shard_map/ppermute | solution.py:630
  161.4 18.4 %copy-start.6 = (f32[4,4,512]{2,1,0:T(4,128)S(1)}, f32[4,4,512]{2,1,0:T(4,128)}, u32[]{:S(2)}) copy-start(f32[4,4,512]{2,1,0:T(4,128)} %attn.3) | copy-start | bytes 98308
  161.4 18.4 %copy-start.7 = (f32[4,2048]{1,0:T(4,128)S(1)}, f32[4,2048]{1,0:T(4,128)}, u32[]{:S(2)}) copy-start(f32[4,2048]{1,0:T(4,128)} %up.3) | copy-start | bytes 98308
  161.4 18.4 %copy-start.8 = (f32[16,512]{1,0:T(8,128)S(1)}, f32[16,512]{1,0:T(8,128)}, u32[]{:S(2)}) copy-start(f32[16,512]{1,0:T(8,128)} %down.3) | copy-start | bytes 98308
where the time goes:
time: 181 us
  blocking collectives  130 us (72%)
  Pallas kernels  26.8 us (15%)
  starting transfers between devices  15.3 us (8%)
  waiting for transfers between devices  7.43 us (4%)
    all_to_all x3, blocking collectives, to_chips(): return lax.all_to_all(value, CHIPS, 0, 0, tiled=True)  121 us
    pallas_call x13, Pallas kernels, call(): pl.pallas_call(kernel, out_shape=shapes, in_specs=spec, out_specs=[pl.Blo...  26.8 us
    ppermute x8, starting transfers between devices, swap(): return lax.ppermute(value, 'c', [(0, 1), (1, 0)])  9.76 us
    all_to_all x1, blocking collectives, body(): orth = lax.all_to_all(orth, ('y', 'c'), 0, 0, tiled=True)  8.89 us
    all_to_all x1, starting transfers between devices, to_chips(): return lax.all_to_all(value, CHIPS, 0, 0, tiled=True)  5.52 us
    all_to_all x1, waiting for transfers between devices, to_chips(): return lax.all_to_all(value, CHIPS, 0, 0, tiled=True)  5.18 us
  transfers between devices with their start and end apart: 9, of which 5 were waited for; matrix products, arithmetic and copies ran while one was open for 0% of the time, Pallas kernels for 7%

commit v1 on v0

--- a/solution.py
+++ b/solution.py
@@ -530,9 +530,9 @@
     rows_scr[...] = NEWTON_FIRST * rows + NEWTON_SECOND * once + NEWTON_THIRD * twice
 
     def send(k, value):
-        value = value.astype(BF).reshape(4, 8, D)
-        out[:, 0, :, D * k : D * (k + 1)] = value
-        out[:, 1, :, D * k : D * (k + 1)] = value
+        value = value.reshape(4, 8, D)
+        for half in range(2):
+            out[:, half, :, D * k : D * (k + 1)] = value[:, 4 * half : 4 * (half + 1)].astype(BF)
 
     @pl.when(role == 2)
     def _():
@@ -601,15 +601,14 @@
 
 
 def update_kernel(
-    core, got, attn, up, down, attn_new, up_new, down_new, attn_copy, up_copy, down_copy, ups, downs
+    got, attn, up, down, attn_new, up_new, down_new, attn_copy, up_copy, down_copy, ups, downs
 ):
-    is_left = core[0] == 0
     keep_share = 1.0 - RATE_MATRIX * DECAY_MATRIX
     for m in range(4):
-        new = attn[m] * keep_share - RATE_MATRIX * rows4(is_left, got[m, :, 0:512].astype(F32))
+        new = attn[m] * keep_share - RATE_MATRIX * got[m, :, 0:512].astype(F32)
         attn_new[m] = new
         attn_copy[m] = new.astype(BF)
-    ups[0:4, :] = rows4(is_left, jnp.concatenate([got[4].astype(F32), got[5].astype(F32)], axis=1))
+    ups[0:4, :] = jnp.concatenate([got[4].astype(F32), got[5].astype(F32)], axis=1)
     ups[4:8, :] = jnp.zeros((4, FF), F32)
     rate = RATE_MATRIX * math.sqrt(max(1.0, FF / D))
     moved = natural(ups)
@@ -619,7 +618,7 @@
     up_copy[...] = up_new[...].astype(BF)
     rate = RATE_MATRIX * math.sqrt(max(1.0, D / FF))
     for q in range(4):
-        step = rows4(is_left, got[6 + q // 2, :, D * (q % 2) : D * (q % 2 + 1)].astype(F32))
+        step = got[6 + q // 2, :, D * (q % 2) : D * (q % 2 + 1)].astype(F32)
         for i in range(4):
             downs[4 * i + q : 4 * i + q + 1, :] = step[i : i + 1]
     down_new[...] = down[...] * keep_share - rate * downs[...]
@@ -747,21 +746,20 @@
     vecs = [t.T for t in (vec_mom, vec_sec, vec_new, vec_copy)]
     (orth,) = call(
         newton_kernel,
-        [((4, 2, 8, 1024), BF)],
+        [((4, 2, 4, 1024), BF)],
         [role, plane, matrix, gram, gram_other],
         scratch=[pltpu.VMEM((D, D), F32), pltpu.VMEM((64, D), F32)],
         smem=(0, 1),
         flops=14 * 3 * 2 * D * D * D,
     )
-    orth = orth.reshape(8, 8, 1024)
+    orth = orth.reshape(8, 4, 1024)
     orth = lax.all_to_all(orth, ("y", "c"), 0, 0, tiled=True)
     news = call(
         update_kernel,
         [((4, 4, D), F32), ((4, FF), F32), ((16, D), F32), ((4, 4, D), BF), ((4, FF), BF), ((16, D), BF)],
-        [core, orth, attn_master, up_master, down_master],
+        [orth, attn_master, up_master, down_master],
         scratch=[pltpu.VMEM((8, FF), F32), pltpu.VMEM((16, D), F32)],
-        smem=(0,),
-        args=range(2, 5),
+        args=range(1, 4),
         results=range(6),
     )
     return (layer_out, input_grad, clip_norm[0, 0], *moms, *news, *vecs)

time: 181 us -> 181 us (level)
  no operation moved by 1% of the time
where the time goes in v1:
time: 181 us; the launch traced here: 180 us
  blocking collectives  130 us (72%)
  Pallas kernels  26.9 us (15%)
  starting transfers between devices  15.3 us (8%)
  waiting for transfers between devices  7.43 us (4%)
    all_to_all x3, blocking collectives, to_chips(): return lax.all_to_all(value, CHIPS, 0, 0, tiled=True)  121 us
    pallas_call x13, Pallas kernels, call(): pl.pallas_call(kernel, out_shape=shapes, in_specs=spec, out_specs=[pl.Blo...  26.9 us
    ppermute x8, starting transfers between devices, swap(): return lax.ppermute(value, 'c', [(0, 1), (1, 0)])  9.76 us
    all_to_all x1, blocking collectives, body(): orth = lax.all_to_all(orth, ('y', 'c'), 0, 0, tiled=True)  8.45 us
    all_to_all x1, starting transfers between devices, to_chips(): return lax.all_to_all(value, CHIPS, 0, 0, tiled=True)  5.52 us
    all_to_all x1, waiting for transfers between devices, to_chips(): return lax.all_to_all(value, CHIPS, 0, 0, tiled=True)  5.18 us
  transfers between devices with their start and end apart: 9, of which 5 were waited for; matrix products, arithmetic and copies ran while one was open for 0% of the time, Pallas kernels for 7%

profile of v1, /device:TPU:1, one launch (start us, length us, event | category | flops | bytes accessed | tf_op | source)
XLA Modules:
  0.0 180.4 jit_solution(18304712926261437625)
XLA Ops:
  0.7 1.2 shard_map.243
  1.8 1.5 collective-permute-start
  3.3 0.9 collective-permute-done.got
  4.2 0.3 shard_map.244
  4.5 0.0 copy-start
  4.6 0.0 copy-start.1
  4.6 0.0 copy-start.12
  4.6 51.8 %all_to_all.25 = bf16[64,8,3200]{2,1,0:T(8,128)(2,1)S(1)} all-to-all(bf16[64,8,3200]{2,1,0:T(8,128)(2,1)S(1)} %get-tuple-element.79), channel_id=1, replica_groups=mesh['x'=4,'z'=4,'y'=4,'c'=2] {'x','z','y'}, dimensions={0} | all-to-all | bytes 6553600 | tf_op jit(solution)/shard_map/all_to_all | solution.py:633
  56.4 0.0 copy-done
  56.4 2.9 %collective-permute-start.1 = (bf16[64,8,3200]{2,1,0:T(8,128)(2,1)S(1)}, bf16[64,8,3200]{2,1,0:T(8,128)(2,1)}, u32[]{:S(2)}, u32[]{:S(2)}) collective-permute-start(bf16[64,8,3200]{2,1,0:T(8,128)(2,1)S(1)} %all_to_all.25), channel_id=1, source_target_pairs={{0,1},{1,0},{2,3},{3,2},{4,5},{5,4},{6,7},{7,6},{8,9},{9,8},{10,11... | collective-permute-start | bytes 9830408 | tf_op jit(solution)/shard_map/ppermute | solution.py:629
  59.2 5.5 %all-to-all-start.1 = ((bf16[64,8,1024]{2,1,0:T(8,128)(2,1)}), bf16[64,8,1024]{2,1,0:T(8,128)(2,1)}, u32[]{:S(2)}, u32[]{:S(2)}) async-start(bf16[64,8,1024]{2,1,0:T(8,128)(2,1)} %copy-done), calls=%async_computation.1 | async-start | bytes 2097152 | tf_op jit(solution)/shard_map/all_to_all | solution.py:633
  64.8 0.1 collective-permute-done.1
  64.8 0.0 copy-done.1
  64.8 0.0 copy-done.12
  64.8 0.0 copy-start.2
  64.8 4.4 %shard_map.245 = (bf16[128,512]{1,0:T(8,128)(2,1)S(1)}, bf16[128,512]{1,0:T(8,128)(2,1)S(1)}, bf16[128,512]{1,0:T(8,128)(2,1)S(1)}, f32[4,256,128]{2,1,0:T(8,128...) custom-call(s32[1]{0:T(128)} %bitcast.core, ...), custom_call_target="tpu_custom_call" | custom-call | flops 536870912 | bytes 6685188 | tf_op jit(solution)/shard_map/pallas_call | solution.py:55
  69.2 0.5 collective-permute-start.3
  69.7 0.0 copy-done.2
  69.7 3.9 %shard_map.246 = (bf16[128,512]{1,0:T(8,128)(2,1)}, f32[128,512]{1,0:T(8,128)S(1)}, bf16[4,128,512]{2,1,0:T(8,128)(2,1)S(1)}, bf16[128,2560]{1,0:T(8,128)(2,1)S(...) custom-call(s32[1]{0:T(128)} %bitcast.core, bf16[128,512]{1,0:T(8,128)(2,1)S(1)} %copy-done.1, ...), custom_call_target="tpu_custom_call" | custom-call | flops 1207959552 | bytes 10912260 | tf_op jit(solution)/shard_map/pallas_call | solution.py:55
  73.6 0.1 collective-permute-start.2
  73.7 0.4 collective-permute-start.4
  74.1 1.3 shard_map.247
  75.4 0.3 collective-permute-done.2.got
  75.7 0.0 collective-permute-done.4.vg_other
  75.7 0.0 collective-permute-done.3.acts_other
  75.8 1.2 shard_map.248
  76.9 5.2 %all-to-all-done.1 = bf16[64,8,1024]{2,1,0:T(8,128)(2,1)} async-done(((bf16[64,8,1024]{2,1,0:T(8,128)(2,1)}), bf16[64,8,1024]{2,1,0:T(8,128)(2,1)}, u32[]{:S(2)}, u32[]{:S(2)}) %all-to-all-start.1) | async-done | bytes 1048608 | tf_op jit(solution)/shard_map/all_to_all | solution.py:633
  82.1 45.0 %all_to_all.26.got = bf16[64,8,3200]{2,1,0:T(8,128)(2,1)S(1)} all-to-all(bf16[64,8,3200]{2,1,0:T(8,128)(2,1)S(1)} %bitcast.20), channel_id=1, replica_groups=mesh['x'=4,'z'=4,'y'=4,'c'=2] {'x','z','y'}, dimensions={0} | all-to-all | bytes 6553600 | tf_op jit(solution)/shard_map/all_to_all | solution.py:633
  127.1 0.6 shard_map.249
  127.7 24.7 %all_to_all.27 = bf16[64,8,1152]{2,1,0:T(8,128)(2,1)S(1)} all-to-all(bf16[64,8,1152]{2,1,0:T(8,128)(2,1)S(1)} %get-tuple-element.105), channel_id=1, replica_groups=mesh['x'=4,'z'=4,'y'=4,'c'=2] {'x','z','y'}, dimensions={0} | all-to-all | bytes 2359296 | tf_op jit(solution)/shard_map/all_to_all | solution.py:633
  152.4 0.0 copy-start.3
  152.4 0.0 copy-start.4
  152.4 0.0 copy-start.5
  152.4 0.0 copy-start.9
  152.4 0.0 copy-start.10
  152.4 0.0 copy-start.11
  152.5 3.8 %collective-permute-start.6 = (f32[8,3200]{1,0:T(8,128)S(1)}, f32[8,3200]{1,0:T(8,128)S(1)}, u32[]{:S(2)}, u32[]{:S(2)}) collective-permute-start(f32[8,3200]{1,0:T(8,128)S(1)} %get-tuple-element.109.grads), channel_id=1, source_target_pairs={{0,1},{1,0},{2,3},{3,2},{4,5},{5,4},{6,7},{7,6},{8,9},{9,8},{10,11... | collective-permute-start | bytes 307208 | tf_op jit(solution)/shard_map/ppermute | solution.py:629
  156.3 0.2 shard_map.250.note
  156.5 0.1 collective-permute-start.5
  156.6 1.2 shard_map.251.mom
  157.8 0.0 collective-permute-done.5.note_other
  157.8 0.0 collective-permute-done.6.grads_other
  157.8 1.2 shard_map.252
  159.0 0.5 collective-permute-start.7
  159.5 0.0 copy-done.3
  159.5 0.0 copy-done.4
  159.5 0.0 copy-done.5
  159.5 0.0 copy-done.9
  159.5 0.0 copy-done.10
  159.5 0.0 copy-done.11
  159.5 0.9 shard_map.253
  160.5 0.9 collective-permute-done.7.gram_other
  161.4 0.0 copy-start.6
  161.4 0.0 copy-start.7
  161.4 0.0 copy-start.8
  161.4 9.5 %shard_map.254 = bf16[4,2,4,1024]{3,2,1,0:T(4,128)(2,1)S(1)} custom-call(s32[1]{0:T(128)} %bitcast.1.role_ref, s32[1]{0:T(128)} %bitcast.2.plane_ref, bf16[2,512,512]{2,1,0:T(8,128)(2,1)S(1)} %get-tuple-element.124.matrix, f32[776,256]{1,0:T(8,128)S(1)} %get-tuple-element.114.gram_own, f32[776,256]{1,0:T(8,128)S(1)} %collective-permute-done.7.gram_other), custom_call_target="tpu_custom_call" | custom-call | flops 11274289152 | bytes 2637832 | tf_op jit(solution)/shard_map/pallas_call | solution.py:55
  171.0 8.5 %all_to_all.28.got = bf16[8,4,1024]{2,1,0:T(4,128)(2,1)S(1)} all-to-all(bf16[8,4,1024]{2,1,0:T(4,128)(2,1)S(1)} %bitcast.23), channel_id=1, replica_groups=mesh['x'=4,'z'=4,'y'=4,'c'=2] {'y','c'}, dimensions={0} | all-to-all | bytes 131072 | tf_op jit(solution)/shard_map/all_to_all | solution.py:756
  179.4 0.0 copy-done.6
  179.4 0.0 copy-done.7
  179.4 0.0 copy-done.8
  179.4 0.9 shard_map.255
Async XLA Ops:
  1.8 2.4 %collective-permute-start = (bf16[8,3200]{1,0:T(8,128)(2,1)S(1)}, bf16[8,3200]{1,0:T(8,128)(2,1)S(1)}, u32[]{:S(2)}, u32[]{:S(2)}) collective-permute-start(bf16[8,3200]{1,0:T(8,128)(2,1)S(1)} %get-tuple-element.78), channel_id=1, source_target_pairs={{0,1},{1,0},{2,3},{3,2},{4,5},{5,4},{6,7},{7,6},{8,9},{9,8},{10,11... | collective-permute-start | bytes 153608 | tf_op jit(solution)/shard_map/ppermute | solution.py:629
  4.5 51.8 %copy-start = (bf16[64,8,1024]{2,1,0:T(8,128)(2,1)}, bf16[64,8,1024]{2,1,0:T(8,128)(2,1)S(1)}, u32[]{:S(2)}) copy-start(bf16[64,8,1024]{2,1,0:T(8,128)(2,1)S(1)} %get-tuple-element.103) | copy-start | bytes 3145732
  4.6 60.3 %copy-start.1 = (bf16[128,512]{1,0:T(8,128)(2,1)S(1)}, bf16[128,512]{1,0:T(8,128)(2,1)}, u32[]{:S(2)}) copy-start(bf16[128,512]{1,0:T(8,128)(2,1)} %x.3) | copy-start | bytes 393220
  4.6 60.3 %copy-start.12 = (s32[1,128]{1,0:T(1,128)S(1)}, s32[1,128]{1,0:T(1,128)}, u32[]{:S(2)}) copy-start(s32[1,128]{1,0:T(1,128)} %seg.1) | copy-start | bytes 1540
  56.4 8.5 %collective-permute-start.1 = (bf16[64,8,3200]{2,1,0:T(8,128)(2,1)S(1)}, bf16[64,8,3200]{2,1,0:T(8,128)(2,1)}, u32[]{:S(2)}, u32[]{:S(2)}) collective-permute-start(bf16[64,8,3200]{2,1,0:T(8,128)(2,1)S(1)} %all_to_all.25), channel_id=1, source_target_pairs={{0,1},{1,0},{2,3},{3,2},{4,5},{5,4},{6,7},{7,6},{8,9},{9,8},{10,11... | collective-permute-start | bytes 9830408 | tf_op jit(solution)/shard_map/ppermute | solution.py:629
  59.2 22.9 %all-to-all-start.1 = ((bf16[64,8,1024]{2,1,0:T(8,128)(2,1)}), bf16[64,8,1024]{2,1,0:T(8,128)(2,1)}, u32[]{:S(2)}, u32[]{:S(2)}) async-start(bf16[64,8,1024]{2,1,0:T(8,128)(2,1)} %copy-done), calls=%async_computation.1 | async-start | bytes 2097152 | tf_op jit(solution)/shard_map/all_to_all | solution.py:633
  64.8 4.9 %copy-start.2 = (bf16[128,512]{1,0:T(8,128)(2,1)S(1)}, bf16[128,512]{1,0:T(8,128)(2,1)}, u32[]{:S(2)}) copy-start(bf16[128,512]{1,0:T(8,128)(2,1)} %cot.1) | copy-start | bytes 393220
  69.2 6.5 %collective-permute-start.3 = (bf16[128,3328]{1,0:T(8,128)(2,1)S(1)}, bf16[128,3328]{1,0:T(8,128)(2,1)S(1)}, u32[]{:S(2)}, u32[]{:S(2)}) collective-permute-start(bf16[128,3328]{1,0:T(8,128)(2,1)S(1)} %get-tuple-element.83.acts_sent), channel_id=1, source_target_pairs={{0,1},{1,0},{2,3},{3,2},{4,5},{5,4},{6,7},{7,6},{8,9},{9,8},{10,11... | collective-permute-start | bytes 2555912 | tf_op jit(solution)/shard_map/ppermute | solution.py:629
  73.6 2.1 %collective-permute-start.2 = (bf16[128,2560]{1,0:T(8,128)(2,1)S(1)}, bf16[128,2560]{1,0:T(8,128)(2,1)S(1)}, u32[]{:S(2)}, u32[]{:S(2)}) collective-permute-start(bf16[128,2560]{1,0:T(8,128)(2,1)S(1)} %get-tuple-element.95), channel_id=1, source_target_pairs={{0,1},{1,0},{2,3},{3,2},{4,5},{5,4},{6,7},{7,6},{8,9},{9,8},{10,11... | collective-permute-start | bytes 1966088 | tf_op jit(solution)/shard_map/ppermute | solution.py:629
  73.7 2.0 %collective-permute-start.4 = (f32[16,512]{1,0:T(8,128)S(1)}, f32[16,512]{1,0:T(8,128)S(1)}, u32[]{:S(2)}, u32[]{:S(2)}) collective-permute-start(f32[16,512]{1,0:T(8,128)S(1)} %get-tuple-element.102.vg), channel_id=1, source_target_pairs={{0,1},{1,0},{2,3},{3,2},{4,5},{5,4},{6,7},{7,6},{8,9},{9,8},{10,11... | collective-permute-start | bytes 98312 | tf_op jit(solution)/shard_map/ppermute | solution.py:629
  152.4 7.1 %copy-start.3 = (f32[4,4,512]{2,1,0:T(4,128)S(1)}, f32[4,4,512]{2,1,0:T(4,128)}, u32[]{:S(2)}) copy-start(f32[4,4,512]{2,1,0:T(4,128)} %attn_m.3) | copy-start | bytes 98308
  152.4 7.1 %copy-start.4 = (f32[4,2048]{1,0:T(4,128)S(1)}, f32[4,2048]{1,0:T(4,128)}, u32[]{:S(2)}) copy-start(f32[4,2048]{1,0:T(4,128)} %up_m.3) | copy-start | bytes 98308
  152.4 7.1 %copy-start.5 = (f32[16,512]{1,0:T(8,128)S(1)}, f32[16,512]{1,0:T(8,128)}, u32[]{:S(2)}) copy-start(f32[16,512]{1,0:T(8,128)} %down_m.3) | copy-start | bytes 98308
  152.4 7.1 %copy-start.9 = (f32[12,4]{0,1:T(4,128)S(1)}, f32[12,4]{0,1:T(4,128)}, u32[]{:S(2)}) copy-start(f32[12,4]{0,1:T(4,128)} %param.18) | copy-start | bytes 580
  152.4 7.1 %copy-start.10 = (f32[12,4]{0,1:T(4,128)S(1)}, f32[12,4]{0,1:T(4,128)}, u32[]{:S(2)}) copy-start(f32[12,4]{0,1:T(4,128)} %param.22) | copy-start | bytes 580
  152.4 7.1 %copy-start.11 = (f32[12,4]{0,1:T(4,128)S(1)}, f32[12,4]{0,1:T(4,128)}, u32[]{:S(2)}) copy-start(f32[12,4]{0,1:T(4,128)} %param.23) | copy-start | bytes 580
  152.5 5.4 %collective-permute-start.6 = (f32[8,3200]{1,0:T(8,128)S(1)}, f32[8,3200]{1,0:T(8,128)S(1)}, u32[]{:S(2)}, u32[]{:S(2)}) collective-permute-start(f32[8,3200]{1,0:T(8,128)S(1)} %get-tuple-element.109.grads), channel_id=1, source_target_pairs={{0,1},{1,0},{2,3},{3,2},{4,5},{5,4},{6,7},{7,6},{8,9},{9,8},{10,11... | collective-permute-start | bytes 307208 | tf_op jit(solution)/shard_map/ppermute | solution.py:629
  156.5 1.3 collective-permute-start.5
  159.0 2.4 %collective-permute-start.7 = (f32[776,256]{1,0:T(8,128)S(1)}, f32[776,256]{1,0:T(8,128)S(1)}, u32[]{:S(2)}, u32[]{:S(2)}) collective-permute-start(f32[776,256]{1,0:T(8,128)S(1)} %get-tuple-element.114.gram_own), channel_id=1, source_target_pairs={{0,1},{1,0},{2,3},{3,2},{4,5},{5,4},{6,7},{7,6},{8,9},{9,8},{10,11... | collective-permute-start | bytes 2383880 | tf_op jit(solution)/shard_map/ppermute | solution.py:629
  161.4 18.0 %copy-start.6 = (f32[4,4,512]{2,1,0:T(4,128)S(1)}, f32[4,4,512]{2,1,0:T(4,128)}, u32[]{:S(2)}) copy-start(f32[4,4,512]{2,1,0:T(4,128)} %attn.3) | copy-start | bytes 98308
  161.4 18.0 %copy-start.7 = (f32[4,2048]{1,0:T(4,128)S(1)}, f32[4,2048]{1,0:T(4,128)}, u32[]{:S(2)}) copy-start(f32[4,2048]{1,0:T(4,128)} %up.3) | copy-start | bytes 98308
  161.4 18.0 %copy-start.8 = (f32[16,512]{1,0:T(8,128)S(1)}, f32[16,512]{1,0:T(8,128)}, u32[]{:S(2)}) copy-start(f32[16,512]{1,0:T(8,128)} %down.3) | copy-start | bytes 98308
